TPU v7x, 512 devices: a whole 4x8x8 slice. The times are simulated.
512 devices in a mesh: dp: 16 (over x, z_lo, core), fsdp: 32 (over y, z_hi).
Axes of the slice: x: 4, y: 8, z: 8 (z_hi: 4, z_lo: 2; z = z_hi * 2 + z_lo), core: 2. Of those that a mesh axis runs over, the one named last changes fastest.
Arguments:
- tokens: bfloat16 [2048, 4096], P(('dp', 'fsdp')), may hold values from -6 to 6
- cotangent: bfloat16 [2048, 4096], P(('dp', 'fsdp')), may hold values from -6 to 6
- w_in: bfloat16 [1152, 128, 128], P('fsdp'), may hold values from -0.1875 to 0.1875
- w_out: bfloat16 [1152, 128, 128], P('fsdp'), may hold values from -0.09375 to 0.09375
- in_rows: int32 [1152], P('fsdp'), may hold values from -1 to 127, as said below
- in_cols: int32 [1152], P('fsdp'), may hold values from -1 to 31, as said below
- out_rows: int32 [1152], P('fsdp'), may hold values from -1 to 127, as said below
- out_cols: int32 [1152], P('fsdp'), may hold values from -1 to 31, as said below
Outputs:
- mixed: bfloat16 [2048, 4096], P(('dp', 'fsdp'))
- input_grad: bfloat16 [2048, 4096], P(('dp', 'fsdp'))
- in_grad: bfloat16 [1152, 128, 128], P('fsdp')
- out_grad: bfloat16 [1152, 128, 128], P('fsdp')
Inputs may be any that keep to these rules, and one draw needn't show every extreme that they name: `in_rows`: slot s lies on fsdp device s // 36. A live slot names a hidden panel r with r // 4 equal to that device; -1 marks an empty slot, and empty slots follow the live ones of their device. No (panel, column block) pair is named twice. On some device all 36 slots are live, on every device at least 24. `in_cols`: -1 exactly where in_rows is -1. `out_rows`: as in_rows, for w_out. `out_cols`: -1 exactly where out_rows is -1.
All inputs are finite; a program needn't handle non-finite values.
Results may differ from a plain program's by a relative error of at most 0.025.
Values may be sent and summed in bfloat16 or wider, within the bound.
A program may use at most 64 MiB of HBM per device.

v0:
```python
import jax
import jax.numpy as jnp
from jax import lax
from jax.sharding import PartitionSpec as P

FF = 16384


def gelu_slope(values):
    cdf = 0.5 * (1.0 + jax.scipy.special.erf(values * 0.7071067811865476))
    return cdf + values * jnp.exp(-0.5 * values * values) * 0.3989422804014327


def slot_tables(slot_rows, slot_cols, per_dev):
    is_live = slot_rows >= 0
    safe_panel = jnp.where(is_live, slot_rows % per_dev, 0)
    safe_column = jnp.where(is_live, slot_cols, 0)
    return (is_live, safe_panel, safe_column)


def pick_blocks(values, slot_index, group_count):
    shaped = values.reshape(values.shape[0], group_count, 128)
    return jnp.take(shaped, slot_index, axis=1)


def fold_slots(is_live, target, contrib, count):
    selector = jnp.logical_and(
        target[:, None] == jnp.arange(count, dtype=jnp.int32)[None, :], is_live[:, None]
    )
    selector = selector.astype(jnp.float32)
    summed = jnp.einsum("stf,sp->tpf", contrib, selector, precision=lax.Precision.HIGHEST)
    return summed.reshape(summed.shape[0], -1)


def local(tokens, cotangent, w_in, w_out, in_rows, in_cols, out_rows, out_cols):
    nfsdp = lax.axis_size("fsdp")
    per_dev = FF // 128 // nfsdp
    width = tokens.shape[1]
    ncol = width // 128
    in_live, in_panel, in_column = slot_tables(in_rows, in_cols, per_dev)
    out_live, out_panel, out_column = slot_tables(out_rows, out_cols, per_dev)
    gathered = lax.all_gather(tokens, "fsdp", axis=0, tiled=True)
    x_pick = pick_blocks(gathered, in_column, ncol)
    pre_act = fold_slots(
        in_live,
        in_panel,
        jnp.einsum("tsd,sfd->stf", x_pick, w_in, preferred_element_type=jnp.float32),
        per_dev,
    )
    hidden = jax.nn.gelu(pre_act, approximate=False).astype(jnp.bfloat16)
    h_pick = pick_blocks(hidden, out_panel, per_dev)
    row_part = h_pick
    contrib = jnp.einsum("tsf,sfd->std", row_part, w_out, preferred_element_type=jnp.float32)
    mixed = lax.psum_scatter(
        fold_slots(out_live, out_column, contrib, ncol).astype(jnp.bfloat16),
        "fsdp",
        scatter_dimension=0,
        tiled=True,
    )
    cot_rows = lax.all_gather(cotangent, "fsdp", axis=0, tiled=True)
    c_pick = pick_blocks(cot_rows, out_column, ncol)
    d_hidden = fold_slots(
        out_live,
        out_panel,
        jnp.einsum("tsd,sfd->stf", c_pick, w_out, preferred_element_type=jnp.float32),
        per_dev,
    )
    d_pre = (d_hidden * gelu_slope(pre_act)).astype(jnp.bfloat16)
    d_pick = pick_blocks(d_pre, in_panel, per_dev)
    grad_out = jnp.einsum("tsf,tsd->sfd", h_pick, c_pick, preferred_element_type=jnp.float32)
    grad_out = jnp.where(out_live[:, None, None], grad_out, 0.0)
    row_part = d_pick
    contrib = jnp.einsum("tsf,sfd->std", row_part, w_in, preferred_element_type=jnp.float32)
    input_grad = lax.psum_scatter(
        fold_slots(in_live, in_column, contrib, ncol).astype(jnp.bfloat16),
        "fsdp",
        scatter_dimension=0,
        tiled=True,
    )
    grad_in = jnp.einsum("tsf,tsd->sfd", d_pick, x_pick, preferred_element_type=jnp.float32)
    grad_in = jnp.where(in_live[:, None, None], grad_in, 0.0)
    out_total, in_total = (
        lax.psum(grad_out.astype(jnp.bfloat16), "dp").astype(jnp.float32),
        lax.psum(grad_in.astype(jnp.bfloat16), "dp").astype(jnp.float32),
    )
    return (mixed, input_grad, in_total.astype(jnp.bfloat16), out_total.astype(jnp.bfloat16))


def solution(mesh):
    placed = (
        P(("dp", "fsdp"), None),
        P(("dp", "fsdp"), None),
        P("fsdp", None, None),
        P("fsdp", None, None),
        P("fsdp"),
        P("fsdp"),
        P("fsdp"),
        P("fsdp"),
    )
    return jax.shard_map(
        local,
        mesh=mesh,
        in_specs=placed,
        out_specs=(
            P(("dp", "fsdp"), None),
            P(("dp", "fsdp"), None),
            P("fsdp", None, None),
            P("fsdp", None, None),
        ),
        check_vma=False,
    )
```

profile of v0, /device:TPU:8, one launch (start us, length us, event | category | flops | bytes accessed | tf_op | source)
XLA Modules:
  0.0 687.5 jit_solution(2108964944030363270)
XLA Ops:
  7.2 0.0 copy-start
  7.2 0.0 all-gather.5.cloned.1.call-start
  7.2 0.7 all-gather.5.cloned.1.call-update
  7.9 0.0 all-gather.7.cloned.1.call-start
  8.0 0.7 all-gather.7.cloned.1.call-update
  8.7 0.0 all-reduce.7.cloned.1.call-start
  8.7 0.7 compare_and_fusion
  9.4 0.7 compare_and_fusion.1
  10.1 0.0 copy-start.5
  10.1 0.0 copy-start.7
  10.2 88.5 %all-gather.5.cloned.1.call-done = bf16[32,4,4096]{2,1,0:T(4,128)(2,1)} async-done(((bf16[1,4,4096]{2,1,0:T(4,128)(2,1)}), bf16[32,4,4096]{2,1,0:T(4,128)(2,1)}) %all-gather.5.cloned.1.call-update) | async-done | bytes 1048592 | tf_op jit(solution)/shard_map/all_gather | solution.py:42
  98.8 2.1 reshape.40
  100.9 0.4 copy.38
  101.3 81.3 %all-gather.7.cloned.1.call-done = bf16[32,4,4096]{2,1,0:T(4,128)(2,1)} async-done(((bf16[1,4,4096]{2,1,0:T(4,128)(2,1)}), bf16[32,4,4096]{2,1,0:T(4,128)(2,1)}) %all-gather.7.cloned.1.call-update) | async-done | bytes 1048592 | tf_op jit(solution)/shard_map/all_gather | solution.py:60
  182.6 2.9 reshape.41
  185.5 1.6 copy.42
  187.2 1.8 gather_fusion
  189.0 0.0 copy-done
  189.0 2.3 fusion.24
  191.2 3.0 fusion.6
  194.2 0.8 gather_fusion.2
  195.0 0.0 copy-done.5
  195.0 2.3 fusion.18
  197.2 0.0 copy-start.4
  197.2 2.3 fusion.2
  199.5 0.0 copy-done.4
  199.5 0.7 fusion.34
  200.2 1.8 gather_fusion.3
  202.0 1.8 fusion.15
  203.8 2.8 fusion.11
  206.6 1.4 copy.69
  208.0 1.8 gather_fusion.1
  209.8 0.0 copy-done.7
  209.8 2.3 fusion.21
  212.2 2.8 fusion.8
  215.0 1.5 copy.70
  216.4 0.0 copy-start.1
  216.4 0.0 all-reduce.7.cloned.1.call-update
  216.5 0.0 all-reduce.9.cloned.1.call-start
  216.5 1.2 copy-done.1
  217.7 0.0 copy-start.2
  217.7 0.0 copy-start.6
  217.7 0.0 copy-start.8
  217.7 3.2 select_convert_fusion.1
  220.9 0.0 copy-done.2
  220.9 0.0 copy-done.6
  220.9 0.0 copy-done.8
  220.9 1.8 select_convert_fusion
  222.7 0.0 all-reduce.9.cloned.1.call-update
  222.7 1.3 dynamic-slice
  224.6 313.1 %all-reduce.7.cloned.1.call-done = (bf16[128,4096]{1,0:T(8,128)(2,1)}, bf16[128,4096]{1,0:T(8,128)(2,1)}) async-done(((bf16[128,4096]{1,0:T(8,128)(2,1)}, bf16[128,4096]{1,0:T(8,128)(2,1)}), (bf16[128,4096]{1,0:T(8,128)(2,1)}, bf16[128,4096]{1,0:T(8,128)(2,1)})) %all-reduce.7.cloned.1.call-update) | async-done | bytes 2097168
  537.7 1.5 constant_dynamic-slice_fusion
  539.3 138.2 %all-reduce.9.cloned.1.call-done = (bf16[36,128,128]{2,1,0:T(8,128)(2,1)}, bf16[36,128,128]{2,1,0:T(8,128)(2,1)}) async-done(((bf16[36,128,128]{2,1,0:T(8,128)(2,1)}, bf16[36,128,128]{2,1,0:T(8,128)(2,1)}), (bf16[36,128,128]{2,1,0:T(8,128)(2,1)}, bf16[36,128,128]{2,1,0:T(8,128)(2,1)})) %all-reduce.9.cloned.1.call-update) | async-done | bytes 2359312 | tf_op jit(solution)/shard_map/psum | solution.py:84
  677.4 0.0 copy-start.3
  677.4 2.5 copy.75
  679.9 0.0 copy-done.3
  679.9 1.0 copy.76
  (8 shorter events, 0.0 us)
Async XLA Ops:
  7.2 181.8 %copy-start = (bf16[36,128,128]{2,1,0:T(8,128)(2,1)S(1)}, bf16[36,128,128]{2,1,0:T(8,128)(2,1)}, u32[]{:S(2)}) copy-start(bf16[36,128,128]{2,1,0:T(8,128)(2,1)} %param.14) | copy-start | bytes 3538948
  7.2 91.6 %all-gather.5.cloned.1.call-start = ((), (), s32[]{:S(2)}) async-start(), calls=%async_computation | async-start | bytes 1081344 | tf_op jit(solution)/shard_map/all_gather | solution.py:42
  7.9 174.7 %all-gather.7.cloned.1.call-start = ((), (), s32[]{:S(2)}) async-start(), calls=%async_computation.1 | async-start | bytes 1081344 | tf_op jit(solution)/shard_map/all_gather | solution.py:60
  8.7 529.1 %all-reduce.7.cloned.1.call-start = ((), (), s32[]{:S(2)}) async-start(), calls=%async_computation.2 | async-start | bytes 4194304
  10.1 184.9 %copy-start.5 = (pred[36]{0:T(512)(128)(4,1)}, pred[36]{0:T(512)(128)(4,1)S(1)}, u32[]{:S(2)}) copy-start(pred[36]{0:T(512)(128)(4,1)S(1)} %get-tuple-element.12) | copy-start | bytes 112
  10.1 199.7 %copy-start.7 = (pred[36]{0:T(512)(128)(4,1)}, pred[36]{0:T(512)(128)(4,1)S(1)}, u32[]{:S(2)}) copy-start(pred[36]{0:T(512)(128)(4,1)S(1)} %get-tuple-element.21) | copy-start | bytes 112
  197.2 2.3 copy-start.4
  216.4 1.3 copy-start.1
  216.5 461.0 %all-reduce.9.cloned.1.call-start = ((), (), s32[]{:S(2)}) async-start(), calls=%async_computation.3 | async-start | bytes 4718592 | tf_op jit(solution)/shard_map/psum | solution.py:84
  217.7 3.2 copy-start.2
  217.7 3.2 copy-start.6
  217.7 3.2 copy-start.8
  677.4 2.5 copy-start.3
Sparse Core Ops, SparseCore 0:
  11.2 87.5 all-gather.4
  101.9 80.6 all-gather.6
  216.6 321.1 all-reduce.6
  541.4 135.9 all-reduce.8
where the time goes:
time: 688 us; the launch traced here: 687 us
  waiting for transfers between devices  622 us (90%)
  matrix products  24.4 us (4%)
  local copies, waits for them, and re-layouts  23.8 us (3%)
  between operations  14.6 us (2%)
    unnamed x5, waiting for transfers between devices  315 us
    psum x1, waiting for transfers between devices, local(): lax.psum(grad_in.astype(jnp.bfloat16), 'dp').astype(jnp.float32)  138 us
    all_gather x1, waiting for transfers between devices, local(): gathered = lax.all_gather(tokens, 'fsdp', axis=0, tiled=True)  88.5 us
    all_gather x1, waiting for transfers between devices, local(): cot_rows = lax.all_gather(cotangent, 'fsdp', axis=0, tiled=True)  81.3 us
  transfers between devices with their start and end apart: 4, of which 4 were waited for; matrix products, arithmetic and copies ran while one was open for 2% of the time, Pallas kernels for 0%

commit v1 on v0

--- a/solution.py
+++ b/solution.py
@@ -2,8 +2,13 @@
 import jax.numpy as jnp
 from jax import lax
 from jax.sharding import PartitionSpec as P
+from jax.lax import all_gather
 
 FF = 16384
+
+
+def divide_columns(sheet, ax_name):
+    return jnp.sum(all_gather(sheet, ax_name), axis=0)
 
 
 def gelu_slope(values):
@@ -81,7 +86,7 @@
     grad_in = jnp.where(in_live[:, None, None], grad_in, 0.0)
     out_total, in_total = (
         lax.psum(grad_out.astype(jnp.bfloat16), "dp").astype(jnp.float32),
-        lax.psum(grad_in.astype(jnp.bfloat16), "dp").astype(jnp.float32),
+        divide_columns(grad_in.astype(jnp.bfloat16), "dp").astype(jnp.float32),
     )
     return (mixed, input_grad, in_total.astype(jnp.bfloat16), out_total.astype(jnp.bfloat16))
 

time: 688 us -> 791 us (1.15)
  the two profiles are of different devices: /device:TPU:8 before, /device:TPU:1 now
where the time goes in v1:
time: 791 us; the launch traced here: 790 us
  waiting for transfers between devices  714 us (90%)
  matrix products  24.3 us (3%)
  local copies, waits for them, and re-layouts  23.9 us (3%)
  between operations  14.6 us (2%)
  other arithmetic  13.7 us (2%)
    unnamed x6, waiting for transfers between devices  299 us
    all_gather x1, waiting for transfers between devices, divide_columns(): return jnp.sum(all_gather(sheet, ax_name), axis=0)  125 us
    psum x1, waiting for transfers between devices, local(): lax.psum(grad_out.astype(jnp.bfloat16), 'dp').astype(jnp.float32)  122 us
    all_gather x1, waiting for transfers between devices, local(): gathered = lax.all_gather(tokens, 'fsdp', axis=0, tiled=True)  86.8 us
    all_gather x1, waiting for transfers between devices, local(): cot_rows = lax.all_gather(cotangent, 'fsdp', axis=0, tiled=True)  81.3 us
  transfers between devices with their start and end apart: 5, of which 5 were waited for; matrix products, arithmetic and copies ran while one was open for 3% of the time, Pallas kernels for 0%

profile of v1, /device:TPU:1, one launch (start us, length us, event | category | flops | bytes accessed | tf_op | source)
XLA Modules:
  0.0 790.5 jit_solution(13625742948913544367)
XLA Ops:
  7.2 0.0 copy-start
  7.2 0.0 all-gather.9.cloned.1.call-start
  7.2 0.7 all-gather.9.cloned.1.call-update
  7.9 0.0 all-gather.11.cloned.1.call-start
  8.0 0.7 all-gather.11.cloned.1.call-update
  8.7 0.0 all-reduce.8.cloned.1.call-start
  8.7 0.7 compare_and_fusion
  9.4 0.0 copy-start.5
  9.4 0.0 copy-start.4
  9.4 0.7 compare_and_fusion.1
  10.2 86.8 %all-gather.9.cloned.1.call-done = bf16[32,4,4096]{2,1,0:T(4,128)(2,1)} async-done(((bf16[1,4,4096]{2,1,0:T(4,128)(2,1)}), bf16[32,4,4096]{2,1,0:T(4,128)(2,1)}) %all-gather.9.cloned.1.call-update) | async-done | bytes 1048592 | tf_op jit(solution)/shard_map/all_gather | solution.py:47
  97.0 2.1 reshape.40
  99.2 0.4 copy.38
  99.6 81.3 %all-gather.11.cloned.1.call-done = bf16[32,4,4096]{2,1,0:T(4,128)(2,1)} async-done(((bf16[1,4,4096]{2,1,0:T(4,128)(2,1)}), bf16[32,4,4096]{2,1,0:T(4,128)(2,1)}) %all-gather.11.cloned.1.call-update) | async-done | bytes 1048592 | tf_op jit(solution)/shard_map/all_gather | solution.py:65
  180.9 2.9 reshape.41
  183.8 1.6 copy.42
  185.5 1.8 gather_fusion
  187.3 0.0 copy-done.5
  187.3 0.0 copy-done
  187.3 2.3 fusion.24
  189.5 3.0 fusion.6
  192.5 0.8 gather_fusion.2
  193.3 2.3 fusion.18
  195.5 0.0 copy-start.3
  195.5 2.3 fusion.2
  197.8 0.0 copy-done.3
  197.8 0.7 fusion.34
  198.5 1.8 gather_fusion.3
  200.3 0.0 copy-done.4
  200.3 1.8 fusion.15
  202.1 2.8 fusion.11
  204.9 1.5 copy.69
  206.4 1.8 gather_fusion.1
  208.2 2.3 fusion.21
  210.6 2.8 fusion.8
  213.3 1.4 copy.70
  214.7 0.0 copy-start.1
  214.7 0.0 all-reduce.8.cloned.1.call-update
  214.8 0.0 all-gather.7.cloned.1.call-start
  214.8 1.2 copy-done.1
  216.0 3.1 select_convert_fusion.1
  219.1 0.0 copy-start.2
  219.1 0.0 all-gather.7.cloned.1.call-update
  219.1 0.0 all-reduce.6.cloned.1.call-start
  219.2 1.2 copy-done.2
  220.4 1.8 select_convert_fusion
  222.1 0.0 all-reduce.6.cloned.1.call-update
  222.2 1.3 dynamic-slice
  224.1 297.3 %all-reduce.8.cloned.1.call-done = (bf16[128,4096]{1,0:T(8,128)(2,1)}, bf16[128,4096]{1,0:T(8,128)(2,1)}) async-done(((bf16[128,4096]{1,0:T(8,128)(2,1)}, bf16[128,4096]{1,0:T(8,128)(2,1)}), (bf16[128,4096]{1,0:T(8,128)(2,1)}, bf16[128,4096]{1,0:T(8,128)(2,1)})) %all-reduce.8.cloned.1.call-update) | async-done | bytes 2097168
  521.4 1.5 constant_dynamic-slice_fusion
  522.9 124.7 %all-gather.7.cloned.1.call-done = bf16[576,128,128]{2,1,0:T(8,128)(2,1)} async-done(((bf16[36,128,128]{2,1,0:T(8,128)(2,1)}), bf16[576,128,128]{2,1,0:T(8,128)(2,1)}) %all-gather.7.cloned.1.call-update) | async-done | bytes 18874384 | tf_op jit(solution)/shard_map/all_gather | solution.py:11
  647.6 11.6 %reduce_sum.12 = bf16[36,128,128]{2,1,0:T(8,128)(2,1)} reduce(bf16[16,36,128,128]{3,2,1,0:T(8,128)(2,1)} %bitcast.99, bf16[]{:T(256)} %constant.108.clone.1), dimensions={0}, to_apply=%region_2.5 | reduce | flops 8847360 | bytes 20054018 | tf_op jit(solution)/shard_map/reduce_sum | solution.py:11
  659.2 122.3 %all-reduce.6.cloned.1.call-done = bf16[36,128,128]{2,1,0:T(8,128)(2,1)} async-done(((bf16[36,128,128]{2,1,0:T(8,128)(2,1)}), bf16[36,128,128]{2,1,0:T(8,128)(2,1)}) %all-reduce.6.cloned.1.call-update) | async-done | bytes 1179664 | tf_op jit(solution)/shard_map/psum | solution.py:88
  781.5 2.4 copy.74
  (8 shorter events, 0.0 us)
Async XLA Ops:
  7.2 180.1 %copy-start = (bf16[36,128,128]{2,1,0:T(8,128)(2,1)S(1)}, bf16[36,128,128]{2,1,0:T(8,128)(2,1)}, u32[]{:S(2)}) copy-start(bf16[36,128,128]{2,1,0:T(8,128)(2,1)} %param.14) | copy-start | bytes 3538948
  7.2 89.9 %all-gather.9.cloned.1.call-start = ((), (), s32[]{:S(2)}) async-start(), calls=%async_computation.2 | async-start | bytes 1081344 | tf_op jit(solution)/shard_map/all_gather | solution.py:47
  7.9 173.0 %all-gather.11.cloned.1.call-start = ((), (), s32[]{:S(2)}) async-start(), calls=%async_computation.3 | async-start | bytes 1081344 | tf_op jit(solution)/shard_map/all_gather | solution.py:65
  8.7 512.7 %all-reduce.8.cloned.1.call-start = ((), (), s32[]{:S(2)}) async-start(), calls=%async_computation.4 | async-start | bytes 4194304
  9.4 177.9 %copy-start.5 = (pred[36]{0:T(512)(128)(4,1)}, pred[36]{0:T(512)(128)(4,1)S(1)}, u32[]{:S(2)}) copy-start(pred[36]{0:T(512)(128)(4,1)S(1)} %get-tuple-element.23) | copy-start | bytes 112
  9.4 190.9 %copy-start.4 = (pred[36]{0:T(512)(128)(4,1)}, pred[36]{0:T(512)(128)(4,1)S(1)}, u32[]{:S(2)}) copy-start(pred[36]{0:T(512)(128)(4,1)S(1)} %get-tuple-element.8) | copy-start | bytes 112
  195.5 2.3 copy-start.3
  214.7 1.3 copy-start.1
  214.8 432.9 %all-gather.7.cloned.1.call-start = ((), (), s32[]{:S(2)}) async-start(), calls=%async_computation.1 | async-start | bytes 20054016 | tf_op jit(solution)/shard_map/all_gather | solution.py:11
  219.1 1.3 copy-start.2
  219.1 562.4 %all-reduce.6.cloned.1.call-start = ((), (), s32[]{:S(2)}) async-start(), calls=%async_computation | async-start | bytes 2359296 | tf_op jit(solution)/shard_map/psum | solution.py:88
Sparse Core Ops, SparseCore 0:
  11.2 85.8 all-gather.8
  100.2 80.6 all-gather.10
  214.9 306.4 all-reduce.7
  524.2 123.3 all-gather.6
  650.7 130.8 all-reduce.5
